TPU v7x, 32 devices: a whole 2x2x4 slice. The times are simulated.
32 devices in a mesh: leaf: 4 (over z), panel: 8 (over y, x, core).
Axes of the slice: x: 2, y: 2, z: 4, core: 2. Of those that a mesh axis runs over, the one named last changes fastest.
Arguments:
- right_sides: float32 [4, 256, 32, 256], P('leaf', 'panel'), may hold values from -6 to 6
- inverse: float32 [4, 256, 256, 256], P('leaf', 'panel'), as said below
- coupling: float32 [4, 256, 256, 256], P('leaf', 'panel'), may hold values from -0.25 to 0.25
- owner_map: int32 [4, 256, 1], P('leaf', 'panel'), may hold values from 0 to 7; in each aligned block of 32 rows (0 to 31, 32 to 63, ..., all dimensions but the last counted through in order) at most 8 rows name the same one
- parent_slot: int32 [4, 256], P('leaf', 'panel'), may hold values from 0 to 31
Outputs:
- forward_solution: float32 [4, 256, 32, 256], P('leaf', 'panel')
- backward_solution: float32 [4, 256, 32, 256], P('leaf', 'panel')
Inputs may be any that keep to these rules, and one draw needn't show every extreme that they name: `owner_map`: within the 32 supernodes of one device no owner is named more than 8 times, and some owner is named exactly that often; entries of the top level are not read. `inverse`: each block is upper triangular with a positive diagonal.
All inputs are finite; a program needn't handle non-finite values.
Results may differ from a plain program's by a relative error of at most 0.0001.
Values sent between devices are 32-bit elements; how exact they have to be, the bound alone decides.
A program may use at most 128 MiB of HBM per device.

v0:
```python
import jax
import jax.numpy as jnp
from jax import lax
from jax.sharding import PartitionSpec as P


def from_behind(block, axis, distance):
    devices = range(lax.axis_size(axis))
    route = [(i - distance, i) for i in devices if i - distance in devices]
    return lax.ppermute(block, axis, route)


def put_block(whole, piece, active):
    return jnp.where(active, piece, whole)


def body(right_sides, inverse, coupling, owner_map, parent_slot):
    highest = lax.Precision.HIGHEST
    levels = lax.axis_size("leaf")
    panels = lax.axis_size("panel")
    level = lax.axis_index("leaf")
    node_count = right_sides.shape[1]
    total_cols = right_sides.shape[2]
    width = right_sides.shape[3]
    capacity = max(2, 2 * node_count // panels)
    slot_count = panels * capacity
    owners = owner_map[0, :, 0]
    positions = parent_slot[0]
    node_iota = jnp.arange(node_count, dtype=jnp.int32)
    same_owner = owners[:, None] == owners[None, :]
    before = node_iota[None, :] < node_iota[:, None]
    slot_rank = jnp.sum((same_owner & before).astype(jnp.int32), axis=1)
    dest_slot = owners * capacity + slot_rank
    slot_iota = jnp.arange(slot_count, dtype=jnp.int32)
    send_onehot = (slot_iota[:, None] == dest_slot[None, :]).astype(jnp.float32)
    send_ids = jnp.dot(send_onehot, (positions + 1).astype(jnp.float32), precision=highest) - 1.0
    node_float = node_iota.astype(jnp.float32)
    block_count = 1
    turns = levels + block_count - 1
    given = right_sides[0]
    diag_inverse = inverse[0]
    couple_block = coupling[0]
    incoming = jnp.zeros((node_count, total_cols, width), jnp.float32)
    solved = jnp.zeros((node_count, total_cols, width), jnp.float32)
    recv_onehot = jnp.zeros((node_count, slot_count), jnp.float32)
    for turn_index in range(turns):
        blk_index = turn_index - level
        active = (blk_index >= 0) & (blk_index < block_count)
        part_in = incoming
        forward_part = jnp.einsum("nrw,nwv->nrv", given - part_in, diag_inverse, precision=highest)
        solved = put_block(solved, forward_part, active)
        if turn_index < turns - 1:
            updates = jnp.einsum("nrw,nwv->nrv", forward_part, couple_block, precision=highest)
            buffer = jnp.einsum("ts,srw->trw", send_onehot, updates, precision=highest)
            arrived, arrived_ids = (
                lax.all_to_all(buffer, "panel", split_axis=0, concat_axis=0, tiled=True),
                lax.all_to_all(send_ids, "panel", split_axis=0, concat_axis=0, tiled=True),
            )
            arrived, arrived_ids = from_behind((arrived, arrived_ids), "leaf", 1)
            recv_onehot = (arrived_ids[None, :] == node_float[:, None]).astype(jnp.float32)
            summed = jnp.einsum("st,trw->srw", recv_onehot, arrived, precision=highest)
            next_index = blk_index + 1
            next_active = (next_index >= 0) & (next_index < block_count)
            incoming = put_block(incoming, summed, next_active)
    height = levels - 1 - level
    lowered = jnp.zeros((node_count, total_cols, width), jnp.float32)
    result = jnp.zeros((node_count, total_cols, width), jnp.float32)
    for turn_index in range(turns):
        blk_index = turn_index - height
        active = (blk_index >= 0) & (blk_index < block_count)
        part_low = lowered
        backward_part = jnp.einsum(
            "nrw,nvw->nrv", solved - part_low, diag_inverse, precision=highest
        )
        result = put_block(result, backward_part, active)
        if turn_index < turns - 1:
            buffer = jnp.einsum("st,srw->trw", recv_onehot, backward_part, precision=highest)
            arrived = from_behind(buffer, "leaf", -1)
            arrived = lax.all_to_all(arrived, "panel", split_axis=0, concat_axis=0, tiled=True)
            picked = jnp.einsum("ts,trw->srw", send_onehot, arrived, precision=highest)
            parent_terms = jnp.einsum("srv,swv->srw", picked, couple_block, precision=highest)
            next_index = blk_index + 1
            next_active = (next_index >= 0) & (next_index < block_count)
            lowered = put_block(lowered, parent_terms, next_active)
    return (solved[None], result[None])


def solution(mesh):
    in_specs = (
        P("leaf", "panel", None, None),
        P("leaf", "panel", None, None),
        P("leaf", "panel", None, None),
        P("leaf", "panel", None),
        P("leaf", "panel"),
    )
    out_specs = (P("leaf", "panel", None, None), P("leaf", "panel", None, None))
    return jax.shard_map(body, mesh=mesh, in_specs=in_specs, out_specs=out_specs, check_vma=False)
```

profile of v0, /device:TPU:1, one launch (start us, length us, event | category | flops | bytes accessed | tf_op | source)
XLA Modules:
  0.0 642.1 jit_solution(2370571733077318036)
XLA Ops:
  2.2 8.7 %fusion.26 = f32[32,32,256]{2,1,0:T(8,128)S(1)} fusion(f32[1,32,256,256]{3,2,1,0:T(8,128)} %param.6, f32[1,32,32,256]{3,2,1,0:T(8,128)} %param.5), kind=kOutput, calls=%fused_computation.26 | convolution fusion | flops 805306368 | bytes 10485760 | tf_op jit(solution)/shard_map/nrw,nwv->nrv/dot_general | solution.py:50
  10.9 4.9 fusion.10
  15.8 1.7 fusion.70
  18.8 30.5 %all_to_all.44 = f32[64,32,256]{2,1,0:T(8,128)S(1)} all-to-all(f32[64,32,256]{2,1,0:T(8,128)S(1)} %copy.33), channel_id=1, replica_groups=mesh['leaf'=4,'panel'=8] {'panel'}, dimensions={0} | all-to-all | bytes 4194304 | tf_op jit(solution)/shard_map/all_to_all | solution.py:56
  50.5 4.7 collective-permute-start.1
  56.1 4.8 all-to-all-start
  60.9 3.9 all-to-all-done
  66.1 1.9 collective-permute-start
  68.0 29.5 %collective-permute-done = f32[64]{0:T(128)S(1)} collective-permute-done((f32[64]{0:T(128)S(1)}, f32[64]{0:T(128)S(1)}, u32[]{:S(2)}, u32[]{:S(2)}) %collective-permute-start) | collective-permute-done | bytes 288 | tf_op jit(solution)/shard_map/ppermute | solution.py:10
  97.4 2.4 fusion.92
  99.9 7.6 %fusion.24 = f32[32,32,256]{2,1,0:T(8,128)S(1)} fusion(f32[1,32,256,256]{3,2,1,0:T(8,128)} %param.6, f32[1,32,32,256]{3,2,1,0:T(8,128)S(1)} %copy-done.2, f32[32,32,256]{2,0,1:T(8,128)S(1)} %fusion.92, pred[]{:T(512)S(6)} %and.37), kind=kOutput, calls=%fused_computation.24 | convolution fusion | flops 805830656 | bytes 11534337 | tf_op jit(solution)/shard_map/nrw,nwv->nrv/dot_general | solution.py:50
  107.5 7.6 %fusion.8 = f32[32,32,256]{2,1,0:T(8,128)S(1)} fusion(f32[32,32,256]{2,1,0:T(8,128)S(1)} %fusion.24, f32[1,32,256,256]{3,2,1,0:T(8,128)} %param.7), kind=kOutput, calls=%fused_computation.8 | convolution fusion | flops 805306368 | bytes 10485760 | tf_op jit(solution)/shard_map/nrw,nwv->nrv/dot_general | solution.py:53
  115.1 1.7 fusion.68
  118.0 30.0 %all_to_all.45 = f32[64,32,256]{2,1,0:T(8,128)S(1)} all-to-all(f32[64,32,256]{2,1,0:T(8,128)S(1)} %copy.37), channel_id=1, replica_groups=mesh['leaf'=4,'panel'=8] {'panel'}, dimensions={0} | all-to-all | bytes 4194304 | tf_op jit(solution)/shard_map/all_to_all | solution.py:56
  148.0 2.6 copy.38
  150.6 5.9 collective-permute-start.2
  156.6 42.1 %collective-permute-done.2 = f32[64,32,256]{2,0,1:T(8,128)} collective-permute-done((f32[64,32,256]{2,0,1:T(8,128)}, f32[64,32,256]{2,0,1:T(8,128)}, u32[]{:S(2)}, u32[]{:S(2)}) %collective-permute-start.2) | collective-permute-done | bytes 2097184 | tf_op jit(solution)/shard_map/ppermute | solution.py:10
  198.7 2.6 fusion.90
  201.3 8.8 %fusion.22 = f32[32,32,256]{2,1,0:T(8,128)S(1)} fusion(f32[1,32,256,256]{3,2,1,0:T(8,128)} %param.6, f32[1,32,32,256]{3,2,1,0:T(8,128)S(1)} %copy-done.2, f32[32,32,256]{2,0,1:T(8,128)S(1)} %fusion.90, f32[32,32,256]{2,0,1:T(8,128)S(1)} %fusion.92, pred[]{:T(512)S(6)} %and.37, pred[]{:T(512)S(6)} %and.36), kind=kOutput, calls=%fused_computation.22 | convolution fusion | flops 806092800 | bytes 12582914 | tf_op jit(solution)/shard_map/nrw,nwv->nrv/dot_general | solution.py:50
  210.2 4.9 fusion.6
  218.0 30.0 %all_to_all.46 = f32[64,32,256]{2,1,0:T(8,128)S(1)} all-to-all(f32[64,32,256]{2,1,0:T(8,128)S(1)} %copy.41), channel_id=1, replica_groups=mesh['leaf'=4,'panel'=8] {'panel'}, dimensions={0} | all-to-all | bytes 4194304 | tf_op jit(solution)/shard_map/all_to_all | solution.py:56
  248.0 2.6 copy.42
  250.6 5.6 collective-permute-start.3
  256.2 42.4 %collective-permute-done.3 = f32[64,32,256]{2,0,1:T(8,128)} collective-permute-done((f32[64,32,256]{2,0,1:T(8,128)}, f32[64,32,256]{2,0,1:T(8,128)}, u32[]{:S(2)}, u32[]{:S(2)}) %collective-permute-start.3) | collective-permute-done | bytes 2097184 | tf_op jit(solution)/shard_map/ppermute | solution.py:10
  298.6 2.6 fusion.88
  301.2 10.8 %fusion.34 = f32[32,32,256]{2,1,0:T(8,128)S(1)} fusion(f32[1,32,256,256]{3,2,1,0:T(8,128)} %param.6, f32[1,32,32,256]{3,2,1,0:T(8,128)S(1)} %copy-done.2, f32[32,32,256]{2,0,1:T(8,128)S(1)} %fusion.88, f32[32,32,256]{2,1,0:T(8,128)} %copy-done.9, f32[32,32,256]{2,1,0:T(8,128)} %copy-done.8, f32[32,32,256]{2,1,0:T(8,128)} %copy-done.7, pred[]{:T(512)S(6)} %and.38, ...), kind=kOutput, calls=%fused_computation.34 | convolution fusion | flops 807403520 | bytes 16777220 | tf_op jit(solution)/shard_map/nrw,nwv->nrv/dot_general | solution.py:50
  312.0 8.1 %fusion.18 = f32[32,32,256]{2,1,0:T(8,128)S(1)} fusion(f32[32,32,256]{2,1,0:T(8,128)S(1)} %fusion.34, f32[1,32,256,256]{3,2,1,0:T(8,128)S(1)} %bitcast.98), kind=kOutput, calls=%fused_computation.18 | convolution fusion | flops 805306368 | bytes 10485760 | tf_op jit(solution)/shard_map/nrw,nvw->nrv/dot_general | solution.py:72
  323.1 46.5 %collective-permute-done.4 = f32[64,32,256]{2,0,1:T(8,128)S(1)} collective-permute-done((f32[64,32,256]{2,0,1:T(8,128)S(1)}, f32[64,32,256]{2,0,1:T(8,128)S(1)}, u32[]{:S(2)}, u32[]{:S(2)}) %collective-permute-start.4) | collective-permute-done | bytes 2097184 | tf_op jit(solution)/shard_map/ppermute | solution.py:10
  369.6 2.5 copy.45
  372.2 7.1 %all-to-all-start.4 = ((f32[64,32,256]{2,1,0:T(8,128)}), f32[64,32,256]{2,1,0:T(8,128)}, u32[]{:S(2)}, u32[]{:S(2)}) async-start(f32[64,32,256]{2,1,0:T(8,128)} %copy.45), calls=%async_computation.4 | async-start | bytes 4194304 | tf_op jit(solution)/shard_map/all_to_all | solution.py:79
  379.3 23.1 %all-to-all-done.4 = f32[64,32,256]{2,1,0:T(8,128)} async-done(((f32[64,32,256]{2,1,0:T(8,128)}), f32[64,32,256]{2,1,0:T(8,128)}, u32[]{:S(2)}, u32[]{:S(2)}) %all-to-all-start.4) | async-done | bytes 2097184 | tf_op jit(solution)/shard_map/all_to_all | solution.py:79
  402.4 3.6 fusion.32
  406.0 10.3 %fusion.43 = f32[32,32,256]{2,1,0:T(8,128)S(1)} fusion(f32[1,32,256,256]{3,2,1,0:T(8,128)} %param.7, f32[32,32,256]{2,0,1:T(8,128)S(1)} %fusion.32, pred[]{:T(512)S(6)} %and.41), kind=kOutput, calls=%fused_computation.37 | convolution fusion | flops 805568512 | bytes 10485761 | tf_op jit(solution)/shard_map/srv,swv->srw/dot_general | solution.py:81
  416.2 10.4 %fusion.16 = f32[32,32,256]{2,1,0:T(8,128)S(1)} fusion(f32[1,32,256,256]{3,2,1,0:T(8,128)} %param.6, f32[32,32,256]{2,1,0:T(8,128)S(1)} %fusion.34, f32[32,32,256]{2,1,0:T(8,128)S(1)} %fusion.43), kind=kOutput, calls=%fused_computation.16 | convolution fusion | flops 805568512 | bytes 11534336 | tf_op jit(solution)/shard_map/nrw,nvw->nrv/dot_general | solution.py:72
  430.7 44.1 %collective-permute-done.5 = f32[64,32,256]{2,0,1:T(8,128)S(1)} collective-permute-done((f32[64,32,256]{2,0,1:T(8,128)S(1)}, f32[64,32,256]{2,0,1:T(8,128)S(1)}, u32[]{:S(2)}, u32[]{:S(2)}) %collective-permute-start.5) | collective-permute-done | bytes 2097184 | tf_op jit(solution)/shard_map/ppermute | solution.py:10
  474.8 2.5 copy.49
  477.4 9.8 %all-to-all-start.5 = ((f32[64,32,256]{2,1,0:T(8,128)}), f32[64,32,256]{2,1,0:T(8,128)}, u32[]{:S(2)}, u32[]{:S(2)}) async-start(f32[64,32,256]{2,1,0:T(8,128)} %copy.49), calls=%async_computation.5 | async-start | bytes 4194304 | tf_op jit(solution)/shard_map/all_to_all | solution.py:79
  487.2 23.2 %all-to-all-done.5 = f32[64,32,256]{2,1,0:T(8,128)} async-done(((f32[64,32,256]{2,1,0:T(8,128)}), f32[64,32,256]{2,1,0:T(8,128)}, u32[]{:S(2)}, u32[]{:S(2)}) %all-to-all-start.5) | async-done | bytes 2097184 | tf_op jit(solution)/shard_map/all_to_all | solution.py:79
  510.3 3.6 fusion.30
  513.9 11.5 %fusion.46 = f32[32,32,256]{2,1,0:T(8,128)S(1)} fusion(f32[32,32,256]{2,1,0:T(8,128)} %copy-done.10, f32[1,32,256,256]{3,2,1,0:T(8,128)} %param.7, f32[32,32,256]{2,0,1:T(8,128)S(1)} %fusion.30, pred[]{:T(512)S(6)} %and.40), kind=kOutput, calls=%fused_computation.38 | convolution fusion | flops 805568512 | bytes 11534337 | tf_op jit(solution)/shard_map/srv,swv->srw/dot_general | solution.py:81
  525.4 10.0 %fusion.14 = f32[32,32,256]{2,1,0:T(8,128)S(1)} fusion(f32[1,32,256,256]{3,2,1,0:T(8,128)} %param.6, f32[32,32,256]{2,1,0:T(8,128)S(1)} %fusion.34, f32[32,32,256]{2,1,0:T(8,128)S(1)} %fusion.46), kind=kOutput, calls=%fused_computation.14 | convolution fusion | flops 805568512 | bytes 11534336 | tf_op jit(solution)/shard_map/nrw,nvw->nrv/dot_general | solution.py:72
  539.4 44.2 %collective-permute-done.6 = f32[64,32,256]{2,0,1:T(8,128)S(1)} collective-permute-done((f32[64,32,256]{2,0,1:T(8,128)S(1)}, f32[64,32,256]{2,0,1:T(8,128)S(1)}, u32[]{:S(2)}, u32[]{:S(2)}) %collective-permute-start.6) | collective-permute-done | bytes 2097184 | tf_op jit(solution)/shard_map/ppermute | solution.py:10
  583.6 2.5 copy.53
  586.1 9.5 %all-to-all-start.6 = ((f32[64,32,256]{2,1,0:T(8,128)}), f32[64,32,256]{2,1,0:T(8,128)}, u32[]{:S(2)}, u32[]{:S(2)}) async-start(f32[64,32,256]{2,1,0:T(8,128)} %copy.53), calls=%async_computation.6 | async-start | bytes 4194304 | tf_op jit(solution)/shard_map/all_to_all | solution.py:79
  595.7 23.1 %all-to-all-done.6 = f32[64,32,256]{2,1,0:T(8,128)} async-done(((f32[64,32,256]{2,1,0:T(8,128)}), f32[64,32,256]{2,1,0:T(8,128)}, u32[]{:S(2)}, u32[]{:S(2)}) %all-to-all-start.6) | async-done | bytes 2097184 | tf_op jit(solution)/shard_map/all_to_all | solution.py:79
  618.9 3.7 fusion.28
  622.6 10.3 %fusion.52 = f32[32,32,256]{2,1,0:T(8,128)S(1)} fusion(f32[32,32,256]{2,1,0:T(8,128)S(1)} %fusion.34, f32[32,32,256]{2,1,0:T(8,128)S(1)} %fusion.46, f32[1,32,256,256]{3,2,1,0:T(8,128)} %param.7, f32[32,32,256]{2,0,1:T(8,128)S(1)} %fusion.28, pred[]{:T(512)S(6)} %and.39), kind=kOutput, calls=%fused_computation.40 | convolution fusion | flops 805830656 | bytes 12582913 | tf_op jit(solution)/shard_map/srv,swv->srw/dot_general | solution.py:81
  633.0 8.8 %fusion.40 = f32[1,32,32,256]{3,2,1,0:T(8,128)} fusion(f32[32,32,256]{2,1,0:T(8,128)S(1)} %fusion.52, f32[1,32,256,256]{3,2,1,0:T(8,128)S(1)} %bitcast.100, f32[32,32,256]{2,1,0:T(8,128)S(1)} %copy-done.6, f32[32,32,256]{2,1,0:T(8,128)S(1)} %copy-done.4, f32[32,32,256]{2,1,0:T(8,128)S(1)} %fusion.18, pred[]{:T(512)S(6)} %and.42, pred[]{:T(512)S(6)} %and.41, ...), kind=kOutput, calls=%fused_computation.36 | convolution fusion | flops 806354944 | bytes 13631492 | tf_op jit(solution)/shard_map/nrw,nvw->nrv/dot_general | solution.py:72
  (61 shorter events, 21.3 us)
Async XLA Ops:
  2.2 8.7 %copy-start = (f32[1,32,256,256]{3,2,1,0:T(8,128)S(1)}, f32[1,32,256,256]{3,2,1,0:T(8,128)}, u32[]{:S(2)}) copy-start(f32[1,32,256,256]{3,2,1,0:T(8,128)} %param.7) | copy-start | bytes 25165828
  10.9 4.9 copy-start.7
  49.3 5.9 copy-start.12
  50.5 49.4 %copy-start.2 = (f32[1,32,32,256]{3,2,1,0:T(8,128)S(1)}, f32[1,32,32,256]{3,2,1,0:T(8,128)}, u32[]{:S(2)}) copy-start(f32[1,32,32,256]{3,2,1,0:T(8,128)} %param.5) | copy-start | bytes 3145732
  50.5 46.9 %collective-permute-start.1 = (f32[64,32,256]{2,0,1:T(8,128)S(1)}, f32[64,32,256]{2,0,1:T(8,128)}, u32[]{:S(2)}, u32[]{:S(2)}) collective-permute-start(f32[64,32,256]{2,0,1:T(8,128)S(1)} %copy.34), channel_id=1, source_target_pairs={{0,8},{8,16},{16,24},{1,9},{9,17},{17,25},{2,10},{10,18},{18,26},{... | collective-permute-start | bytes 6291464 | tf_op jit(solution)/shard_map/ppermute | solution.py:10
  56.1 8.8 %all-to-all-start = ((f32[8,8,1]{1,2,0:T(1,128)}), f32[8,8,1]{1,2,0:T(1,128)S(1)}, u32[]{:S(2)}, u32[]{:S(2)}) async-start(f32[8,8,1]{1,2,0:T(1,128)} %bitcast.5), calls=%async_computation | async-start | bytes 8192 | tf_op jit(solution)/shard_map/all_to_all | solution.py:57
  66.1 31.3 %collective-permute-start = (f32[64]{0:T(128)S(1)}, f32[64]{0:T(128)S(1)}, u32[]{:S(2)}, u32[]{:S(2)}) collective-permute-start(f32[64]{0:T(128)S(1)} %all_to_all.30), channel_id=1, source_target_pairs={{0,8},{8,16},{16,24},{1,9},{9,17},{17,25},{2,10},{10,18},{18,26},{... | collective-permute-start | bytes 776 | tf_op jit(solution)/shard_map/ppermute | solution.py:10
  107.5 7.6 %copy-start.8 = (f32[32,32,256]{2,1,0:T(8,128)}, f32[32,32,256]{2,1,0:T(8,128)S(1)}, u32[]{:S(2)}) copy-start(f32[32,32,256]{2,1,0:T(8,128)S(1)} %fusion.24) | copy-start | bytes 3145732
  150.6 48.1 %collective-permute-start.2 = (f32[64,32,256]{2,0,1:T(8,128)}, f32[64,32,256]{2,0,1:T(8,128)}, u32[]{:S(2)}, u32[]{:S(2)}) collective-permute-start(f32[64,32,256]{2,0,1:T(8,128)} %copy.38), channel_id=1, source_target_pairs={{0,8},{8,16},{16,24},{1,9},{9,17},{17,25},{2,10},{10,18},{18,26},{... | collective-permute-start | bytes 6291464 | tf_op jit(solution)/shard_map/ppermute | solution.py:10
  198.7 11.5 %slice-start.4 = ((s8[8388608]{0:T(1024)(128)(4,1)}), s8[4194304]{0:T(1024)(128)(4,1)S(1)}, s32[]{:S(2)}) async-start(s8[8388608]{0:T(1024)(128)(4,1)} %bitcast.101), calls=%async_computation.11 | async-start | bytes 8388608
  201.3 8.9 %copy-start.11 = (f32[32,32,256]{2,0,1:T(8,128)}, f32[32,32,256]{2,0,1:T(8,128)S(1)}, u32[]{:S(2)}) copy-start(f32[32,32,256]{2,0,1:T(8,128)S(1)} %fusion.90) | copy-start | bytes 3145732
  201.3 8.9 %slice-start.5 = ((s8[8388608]{0:T(1024)(128)(4,1)}), s8[4194304]{0:T(1024)(128)(4,1)S(1)}, s32[]{:S(2)}) async-start(s8[8388608]{0:T(1024)(128)(4,1)} %bitcast.101), calls=%async_computation.12 | async-start | bytes 8388608
  210.2 4.9 copy-start.9
  250.6 48.0 %collective-permute-start.3 = (f32[64,32,256]{2,0,1:T(8,128)}, f32[64,32,256]{2,0,1:T(8,128)}, u32[]{:S(2)}, u32[]{:S(2)}) collective-permute-start(f32[64,32,256]{2,0,1:T(8,128)} %copy.42), channel_id=1, source_target_pairs={{0,8},{8,16},{16,24},{1,9},{9,17},{17,25},{2,10},{10,18},{18,26},{... | collective-permute-start | bytes 6291464 | tf_op jit(solution)/shard_map/ppermute | solution.py:10
  298.6 13.4 %slice-start = ((s8[8388608]{0:T(1024)(128)(4,1)}), s8[4194304]{0:T(1024)(128)(4,1)S(1)}, s32[]{:S(2)}) async-start(s8[8388608]{0:T(1024)(128)(4,1)} %bitcast.97), calls=%async_computation.7 | async-start | bytes 8388608
  301.2 10.8 %slice-start.1 = ((s8[8388608]{0:T(1024)(128)(4,1)}), s8[4194304]{0:T(1024)(128)(4,1)S(1)}, s32[]{:S(2)}) async-start(s8[8388608]{0:T(1024)(128)(4,1)} %bitcast.97), calls=%async_computation.8 | async-start | bytes 8388608
  312.0 310.6 %copy-start.1 = (f32[32,32,256]{2,1,0:T(8,128)}, f32[32,32,256]{2,1,0:T(8,128)S(1)}, u32[]{:S(2)}) copy-start(f32[32,32,256]{2,1,0:T(8,128)S(1)} %fusion.34) | copy-start | bytes 3145732
  321.8 47.8 %collective-permute-start.4 = (f32[64,32,256]{2,0,1:T(8,128)S(1)}, f32[64,32,256]{2,0,1:T(8,128)S(1)}, u32[]{:S(2)}, u32[]{:S(2)}) collective-permute-start(f32[64,32,256]{2,0,1:T(8,128)S(1)} %fusion.64), channel_id=1, source_target_pairs={{8,0},{16,8},{24,16},{9,1},{17,9},{25,17},{10,2},{18,10},{26,18},{... | collective-permute-start | bytes 6291464 | tf_op jit(solution)/shard_map/ppermute | solution.py:10
  372.2 30.2 %all-to-all-start.4 = ((f32[64,32,256]{2,1,0:T(8,128)}), f32[64,32,256]{2,1,0:T(8,128)}, u32[]{:S(2)}, u32[]{:S(2)}) async-start(f32[64,32,256]{2,1,0:T(8,128)} %copy.45), calls=%async_computation.4 | async-start | bytes 4194304 | tf_op jit(solution)/shard_map/all_to_all | solution.py:79
  416.2 10.5 %copy-start.10 = (f32[32,32,256]{2,1,0:T(8,128)}, f32[32,32,256]{2,1,0:T(8,128)S(1)}, u32[]{:S(2)}) copy-start(f32[32,32,256]{2,1,0:T(8,128)S(1)} %fusion.43) | copy-start | bytes 3145732
  426.7 1.0 copy-start.3
  429.4 45.4 %collective-permute-start.5 = (f32[64,32,256]{2,0,1:T(8,128)S(1)}, f32[64,32,256]{2,0,1:T(8,128)S(1)}, u32[]{:S(2)}, u32[]{:S(2)}) collective-permute-start(f32[64,32,256]{2,0,1:T(8,128)S(1)} %fusion.61), channel_id=1, source_target_pairs={{8,0},{16,8},{24,16},{9,1},{17,9},{25,17},{10,2},{18,10},{26,18},{... | collective-permute-start | bytes 6291464 | tf_op jit(solution)/shard_map/ppermute | solution.py:10
  477.4 32.9 %all-to-all-start.5 = ((f32[64,32,256]{2,1,0:T(8,128)}), f32[64,32,256]{2,1,0:T(8,128)}, u32[]{:S(2)}, u32[]{:S(2)}) async-start(f32[64,32,256]{2,1,0:T(8,128)} %copy.49), calls=%async_computation.5 | async-start | bytes 4194304 | tf_op jit(solution)/shard_map/all_to_all | solution.py:79
  535.4 1.0 copy-start.5
  538.1 45.5 %collective-permute-start.6 = (f32[64,32,256]{2,0,1:T(8,128)S(1)}, f32[64,32,256]{2,0,1:T(8,128)S(1)}, u32[]{:S(2)}, u32[]{:S(2)}) collective-permute-start(f32[64,32,256]{2,0,1:T(8,128)S(1)} %fusion.58), channel_id=1, source_target_pairs={{8,0},{16,8},{24,16},{9,1},{17,9},{25,17},{10,2},{18,10},{26,18},{... | collective-permute-start | bytes 6291464 | tf_op jit(solution)/shard_map/ppermute | solution.py:10
  586.1 32.7 %all-to-all-start.6 = ((f32[64,32,256]{2,1,0:T(8,128)}), f32[64,32,256]{2,1,0:T(8,128)}, u32[]{:S(2)}, u32[]{:S(2)}) async-start(f32[64,32,256]{2,1,0:T(8,128)} %copy.53), calls=%async_computation.6 | async-start | bytes 4194304 | tf_op jit(solution)/shard_map/all_to_all | solution.py:79
  618.9 14.1 %slice-start.2 = ((s8[8388608]{0:T(1024)(128)(4,1)}), s8[4194304]{0:T(1024)(128)(4,1)S(1)}, s32[]{:S(2)}) async-start(s8[8388608]{0:T(1024)(128)(4,1)} %bitcast.99), calls=%async_computation.9 | async-start | bytes 8388608
  622.6 10.4 %slice-start.3 = ((s8[8388608]{0:T(1024)(128)(4,1)}), s8[4194304]{0:T(1024)(128)(4,1)S(1)}, s32[]{:S(2)}) async-start(s8[8388608]{0:T(1024)(128)(4,1)} %bitcast.99), calls=%async_computation.10 | async-start | bytes 8388608
  622.6 10.4 %copy-start.4 = (f32[32,32,256]{2,1,0:T(8,128)S(1)}, f32[32,32,256]{2,1,0:T(8,128)}, u32[]{:S(2)}) copy-start(f32[32,32,256]{2,1,0:T(8,128)} %copy-done.3) | copy-start | bytes 3145732
  622.6 10.4 %copy-start.6 = (f32[32,32,256]{2,1,0:T(8,128)S(1)}, f32[32,32,256]{2,1,0:T(8,128)}, u32[]{:S(2)}) copy-start(f32[32,32,256]{2,1,0:T(8,128)} %copy-done.5) | copy-start | bytes 3145732
where the time goes:
time: 655 us; the launch traced here: 642 us
  waiting for transfers between devices  322 us (49%)
  matrix products  152 us (23%)
  blocking collectives  90.5 us (14%)
  starting transfers between devices  53.2 us (8%)
  local copies, waits for them, and re-layouts  21 us (3%)
    ppermute x7, waiting for transfers between devices, from_behind(): return lax.ppermute(block, axis, route)  249 us
    all_to_all x3, blocking collectives, body(): lax.all_to_all(buffer, 'panel', split_axis=0, concat_axis=0, tiled=True)  90.5 us
    all_to_all x3, waiting for transfers between devices, body(): lax.all_to_all(arrived, 'panel', split_axis=0, concat_axis=0, tiled=True)  69.4 us
    dot_general x4, matrix products, body(): jnp.einsum('nrw,nvw->nrv', solved - part_low, diag_inverse, precision=hig...  37.4 us
    dot_general x4, matrix products, body(): jnp.einsum('nrw,nwv->nrv', given - part_in, diag_inverse, precision=highest)  35.9 us
    dot_general x3, matrix products, body(): jnp.einsum('srv,swv->srw', picked, couple_block, precision=highest)  32.1 us
    all_to_all x3, starting transfers between devices, body(): lax.all_to_all(arrived, 'panel', split_axis=0, concat_axis=0, tiled=True)  26.4 us
    ppermute x7, starting transfers between devices, from_behind(): return lax.ppermute(block, axis, route)  21.9 us
  transfers between devices with their start and end apart: 11, of which 10 were waited for; matrix products, arithmetic and copies ran while one was open for 0% of the time, Pallas kernels for 0%

commit v1 on v0

v1 whole, which is shorter than its diff:
```python
import functools

import jax
import jax.numpy as jnp
from jax import lax
from jax.experimental import pallas as pl
from jax.experimental.pallas import tpu as pltpu
from jax.sharding import PartitionSpec as P

MESH = pl.DeviceIdType.MESH
ROWS = 8
WCHUNK = 4


def split_rows(x):
    high = x.astype(jnp.bfloat16).astype(jnp.float32)
    return jnp.concatenate([high, x - high], axis=0).astype(jnp.bfloat16)


def times(x, weights):
    parts = split_rows(x)
    parts = jnp.concatenate([parts, parts], axis=1)
    out = jnp.dot(parts, weights, preferred_element_type=jnp.float32)
    return out[:ROWS] + out[ROWS:]


def times_transposed(x, weights):
    parts = split_rows(x)
    out = lax.dot_general(parts, weights, (((1,), (1,)), ((), ())), preferred_element_type=jnp.float32)
    half = out.shape[1] // 2
    return (out[:ROWS, :half] + out[ROWS:, :half]) + (out[:ROWS, half:] + out[ROWS:, half:])


def kernel(levels, panels, nodes, blocks, width, cap, *refs):
    meta, given, inverse, coupling, fwd_out, bwd_out = refs[:6]
    refs = list(refs[6:])
    take = lambda count: [refs.pop(0) for _ in range(count)]
    inv32, cpl32, inv, cpl, gbuf, fsol, bsol, upd, prefix, send_up, sums, got_sums, send_down = take(13)
    got_up, got_down, got_above = take(blocks), take(blocks), take(blocks)
    w_sem, g_sem, o_sem, up_s, up_r, z_s, z_r, dn_s, dn_r, b_s, b_r = take(11)

    slots = panels * cap
    m_send, m_order, m_cont, m_pos, m_last, m_slot = 0, slots, 2 * slots, 3 * slots, 4 * slots, 4 * slots + nodes
    level = lax.axis_index("leaf")
    me = lax.axis_index("panel")
    chunk = ROWS
    chunks = nodes // chunk
    wchunks = nodes // WCHUNK
    below_top = level < levels - 1
    above_bottom = level > 0

    def given_copy(b):
        return pltpu.make_async_copy(given.at[0, :, pl.ds(b * ROWS, ROWS), :], gbuf.at[b], g_sem.at[b])

    def weight_copy(which, c):
        source, target = ((inverse, inv32), (coupling, cpl32))[which]
        span = pl.ds(c * WCHUNK, WCHUNK)
        return pltpu.make_async_copy(source.at[0, span], target.at[span], w_sem.at[which, c])

    def out_copy(which, b):
        source, target = ((fsol, fwd_out), (bsol, bwd_out))[which]
        return pltpu.make_async_copy(source.at[b], target.at[0, :, pl.ds(b * ROWS, ROWS), :], o_sem.at[which, b])

    def spread_copy(b, buffer, target, send, recv, owner):
        return pltpu.make_async_remote_copy(
            src_ref=buffer.at[b, pl.ds(owner * cap, cap)], dst_ref=target.at[pl.ds(me * cap, cap)],
            send_sem=send.at[b], recv_sem=recv.at[b], device_id=(level, owner), device_id_type=MESH)

    def up_copy(b, c):
        span = pl.ds(c * chunk, chunk)
        return pltpu.make_async_remote_copy(
            src_ref=sums.at[b, span], dst_ref=got_sums.at[b, span],
            send_sem=z_s.at[b], recv_sem=z_r.at[b, c], device_id=(level + 1, me), device_id_type=MESH)

    def down_copy(b, c):
        span = pl.ds(c * chunk, chunk)
        return pltpu.make_async_remote_copy(
            src_ref=bsol.at[b, span], dst_ref=got_above[b].at[span],
            send_sem=b_s.at[b], recv_sem=b_r.at[b], device_id=(level - 1, me), device_id_type=MESH)

    def wait_bytes(ref, sem):
        pltpu.make_async_copy(ref, ref, sem).wait()

    given_copy(0).start()
    for c in range(wchunks):
        weight_copy(0, c).start()
        weight_copy(1, c).start()
    for b in range(1, blocks):
        given_copy(b).start()

    barrier = pltpu.get_barrier_semaphore()

    def greet(d, carry):
        pl.semaphore_signal(barrier, inc=1, device_id=(level, lax.rem(me + d, panels)), device_id_type=MESH)
        return carry

    lax.fori_loop(1, panels, greet, 0)

    @pl.when(below_top)
    def _():
        pl.semaphore_signal(barrier, inc=1, device_id=(level + 1, me), device_id_type=MESH)

    @pl.when(above_bottom)
    def _():
        pl.semaphore_signal(barrier, inc=1, device_id=(level - 1, me), device_id_type=MESH)

    vertical = jnp.where(below_top, 1, 0) + jnp.where(above_bottom, 1, 0)
    pl.semaphore_wait(barrier, panels - 1 + vertical)

    @pl.when(level == 0)
    def _():
        got_sums[...] = jnp.zeros_like(got_sums)

    prefix[slots] = jnp.zeros((ROWS, width), jnp.float32)

    def forward_nodes(b, first, count):
        for i in range(count):
            n = first + i
            x = times(gbuf[b, n] - got_sums[b, n], inv[n])
            fsol[b, n] = x
            upd[n] = times(x, cpl[n])

    given_copy(0).wait()

    def prepare(c, carry):
        for which, (source, target) in enumerate(((inv32, inv), (cpl32, cpl))):
            weight_copy(which, c).wait()
            for i in range(WCHUNK):
                n = c * WCHUNK + i
                for r in range(0, width, 64):
                    w = source[n, r:r + 64, :]
                    high = w.astype(jnp.bfloat16)
                    target[n, r:r + 64, :] = high
                    target[n, width + r:width + r + 64, :] = (w - high.astype(jnp.float32)).astype(jnp.bfloat16)

        @pl.when(level == 0)
        def _():
            forward_nodes(0, c * WCHUNK, WCHUNK)

        return carry

    lax.fori_loop(0, wchunks, prepare, 0)

    def forward(b):
        if b > 0:
            given_copy(b).wait()

        def one(c, carry):
            @pl.when(above_bottom)
            def _():
                wait_bytes(got_sums.at[b, pl.ds(c * chunk, chunk)], z_r.at[b, c])

            forward_nodes(b, c * chunk, chunk)
            return carry

        lax.fori_loop(0, chunks, one, 0)

    def spread(b, source, base, buffer, target, send, recv):
        for k in range(cap):
            target[me * cap + k] = source[meta[base + me * cap + k]]

        def one(d, carry):
            owner = lax.rem(me + d, panels)
            for k in range(cap):
                buffer[b, owner * cap + k] = source[meta[base + owner * cap + k]]
            spread_copy(b, buffer, target, send, recv, owner).start()
            return carry

        lax.fori_loop(1, panels, one, 0)

    def add_up(b):
        wait_bytes(got_up[b].at[pl.ds(0, slots - cap)], up_r.at[b])

        def run(j8, acc):
            for i in range(8):
                j = j8 * 8 + i
                acc = jnp.where(meta[m_cont + j] > 0, acc, 0.0) + got_up[b][meta[m_order + j]]
                prefix[j] = acc
            return acc

        lax.fori_loop(0, slots // 8, run, jnp.zeros((ROWS, width), jnp.float32))

        def one(c, carry):
            for i in range(chunk):
                m = c * chunk + i
                sums[b, m] = prefix[meta[m_last + m]]
            up_copy(b, c).start()
            return carry

        lax.fori_loop(0, chunks, one, 0)

    def top(b):
        def one(c, carry):
            wait_bytes(got_sums.at[b, pl.ds(c * chunk, chunk)], z_r.at[b, c])
            for i in range(chunk):
                n = c * chunk + i
                x = times(gbuf[b, n] - got_sums[b, n], inv[n])
                fsol[b, n] = x
                bsol[b, n] = times_transposed(x, inv[n])
            down_copy(b, c).start()
            return carry

        lax.fori_loop(0, chunks, one, 0)

    def hand_down(b):
        wait_bytes(got_above[b], b_r.at[b])
        spread(b, got_above[b], m_pos, send_down, got_down[b], dn_s, dn_r)

    def backward(b):
        wait_bytes(got_down[b].at[pl.ds(0, slots - cap)], dn_r.at[b])

        def one(c, carry):
            for i in range(chunk):
                n = c * chunk + i
                low = times_transposed(got_down[b][meta[m_slot + n]], cpl[n])
                bsol[b, n] = times_transposed(fsol[b, n] - low, inv[n])

            @pl.when(above_bottom)
            def _():
                down_copy(b, c).start()

            return carry

        lax.fori_loop(0, chunks, one, 0)
        out_copy(1, b).start()

    @pl.when(below_top)
    def _():
        for b in range(blocks + 1):
            if b < blocks:
                if b == 0:
                    @pl.when(above_bottom)
                    def _():
                        forward(0)
                else:
                    forward(b)
                spread(b, upd, m_send, send_up, got_up[b], up_s, up_r)
                out_copy(0, b).start()
            if b > 0:
                add_up(b - 1)
        for b in range(blocks + 1):
            if b < blocks:
                hand_down(b)
            if b > 0:
                backward(b - 1)
        for b in range(blocks):
            wait_bytes(send_up.at[b, pl.ds(0, slots - cap)], up_s.at[b])
            wait_bytes(send_down.at[b, pl.ds(0, slots - cap)], dn_s.at[b])
            wait_bytes(sums.at[b], z_s.at[b])

    @pl.when(level == levels - 1)
    def _():
        for b in range(blocks):
            if b > 0:
                given_copy(b).wait()
            top(b)
            out_copy(0, b).start()
            out_copy(1, b).start()

    @pl.when(above_bottom)
    def _():
        for b in range(blocks):
            wait_bytes(bsol.at[b], b_s.at[b])

    for b in range(blocks):
        out_copy(0, b).wait()
        out_copy(1, b).wait()


def places(owners, positions, panels, cap):
    nodes = owners.shape[0]
    slots = panels * cap
    i32 = jnp.int32
    node = jnp.arange(nodes, dtype=i32)
    slot = jnp.arange(slots, dtype=i32)
    same = (owners[:, None] == owners[None, :]) & (node[None, :] < node[:, None])
    dest = owners * cap + jnp.sum(same.astype(i32), axis=1)
    hit = slot[:, None] == dest[None, :]
    send = jnp.sum(jnp.where(hit, node[None, :], 0), axis=1)
    ids = nodes - jnp.sum(jnp.where(hit, nodes - positions[None, :], 0), axis=1)
    key = lax.all_to_all(ids, "panel", split_axis=0, concat_axis=0, tiled=True)
    ahead = (key[None, :] < key[:, None]) | ((key[None, :] == key[:, None]) & (slot[None, :] < slot[:, None]))
    rank = jnp.sum(ahead.astype(i32), axis=1)
    placed = rank[None, :] == slot[:, None]
    order = jnp.sum(jnp.where(placed, slot[None, :], 0), axis=1)
    cont = jnp.max(jnp.where(ahead & (key[None, :] == key[:, None]), 1, 0), axis=1)
    cont = jnp.sum(jnp.where(placed, cont[None, :], 0), axis=1)
    mine = key[None, :] == node[:, None]
    last = jnp.max(jnp.where(mine, rank[None, :], -1), axis=1)
    last = jnp.where(last < 0, slots, last)
    return jnp.concatenate([send, order, cont, jnp.minimum(key, nodes - 1), last, dest]).astype(i32)


def body(right_sides, inverse, coupling, owner_map, parent_slot):
    levels = lax.axis_size("leaf")
    panels = lax.axis_size("panel")
    nodes, total_cols, width = right_sides.shape[1:]
    cap = max(2, 2 * nodes // panels)
    slots = panels * cap
    blocks = total_cols // ROWS
    meta = places(owner_map[0, :, 0], parent_slot[0], panels, cap)
    tile = (ROWS, width)
    f32, bf16 = jnp.float32, jnp.bfloat16
    vmem = pltpu.VMEM
    dma = pltpu.SemaphoreType.DMA
    chunks = nodes // ROWS
    scratch = [
        vmem((nodes, width, width), f32), vmem((nodes, width, width), f32),
        vmem((nodes, 2 * width, width), bf16), vmem((nodes, 2 * width, width), bf16),
        vmem((blocks, nodes) + tile, f32), vmem((blocks, nodes) + tile, f32), vmem((blocks, nodes) + tile, f32),
        vmem((nodes,) + tile, f32), vmem((slots + 1,) + tile, f32),
        vmem((blocks, slots) + tile, f32), vmem((blocks, nodes) + tile, f32), vmem((blocks, nodes) + tile, f32),
        vmem((blocks, slots) + tile, f32),
    ]
    scratch += [vmem((slots,) + tile, f32) for _ in range(2 * blocks)]
    scratch += [vmem((nodes,) + tile, f32) for _ in range(blocks)]
    scratch += [
        dma((2, nodes // WCHUNK)), dma((blocks,)), dma((2, blocks)),
        dma((blocks,)), dma((blocks,)), dma((blocks,)), dma((blocks, chunks)),
        dma((blocks,)), dma((blocks,)), dma((blocks,)), dma((blocks,)),
    ]
    out = jax.ShapeDtypeStruct(right_sides.shape, f32)
    anywhere = pl.BlockSpec(memory_space=pl.ANY)
    return pl.pallas_call(
        functools.partial(kernel, levels, panels, nodes, blocks, width, cap),
        out_shape=(out, out),
        in_specs=[pl.BlockSpec(memory_space=pltpu.SMEM), anywhere, anywhere, anywhere],
        out_specs=(anywhere, anywhere),
        scratch_shapes=scratch,
        compiler_params=pltpu.CompilerParams(
            collective_id=0, has_side_effects=True, vmem_limit_bytes=60 * 1024 * 1024
        ),
    )(meta, right_sides, inverse, coupling)


def solution(mesh):
    in_specs = (
        P("leaf", "panel", None, None),
        P("leaf", "panel", None, None),
        P("leaf", "panel", None, None),
        P("leaf", "panel", None),
        P("leaf", "panel"),
    )
    out_specs = (P("leaf", "panel", None, None), P("leaf", "panel", None, None))
    return jax.shard_map(body, mesh=mesh, in_specs=in_specs, out_specs=out_specs, check_vma=False)
```

time: 655 us -> 159 us (0.24); the launches traced: 642 us -> 158 us
  waiting for transfers between devices: 322 us -> 0 us
  matrix products: 152 us -> 0 us
  Pallas kernels: 0 us -> 139 us
  blocking collectives: 90.5 us -> 8.98 us
  starting transfers between devices: 53.2 us -> 0 us
  local copies, waits for them, and re-layouts: 21 us -> 5.96 us
    ppermute x7 -> x0, waiting for transfers between devices: 249 us -> none  [from_behind(): return lax.ppermute(block, axis, route)]
    dot_general x27 -> x0, matrix products: 152 us -> none  [the longest x4 37.4 us: body(): jnp.einsum('nrw,nvw->nrv', solved - part_low, diag_inverse, precision=hig...]
    pallas_call x0 -> x1, Pallas kernels: none -> 139 us  [body(): pl.pallas_call(functools.partial(kernel, levels, panels, nodes, blocks, w...]
    all_to_all x3 -> x1, blocking collectives: 90.5 us -> 8.98 us  [places(): key = lax.all_to_all(ids, 'panel', split_axis=0, concat_axis=0, tiled=True)]
    all_to_all x4 -> x0, waiting for transfers between devices: 73.4 us -> none  [the longest x3 69.4 us: body(): lax.all_to_all(arrived, 'panel', split_axis=0, concat_axis=0, tiled=True)]
    all_to_all x4 -> x0, starting transfers between devices: 31.2 us -> none  [the longest x3 26.4 us: body(): lax.all_to_all(arrived, 'panel', split_axis=0, concat_axis=0, tiled=True)]
    ppermute x7 -> x0, starting transfers between devices: 21.9 us -> none  [from_behind(): return lax.ppermute(block, axis, route)]
    ppermute x3 -> x0, local copies, waits for them, and re-layouts: 7.65 us -> none  [from_behind(): return lax.ppermute(block, axis, route)]
  transfers between devices with their start and end apart: 11 -> 0, of which waited for: 10 -> 0; matrix products, arithmetic and copies ran while one was open for 0% -> 0% of each run, Pallas kernels for 0% -> 0%
where the time goes in v1:
time: 159 us; the launch traced here: 158 us
  Pallas kernels  139 us (87%)
  blocking collectives  8.98 us (6%)
  local copies, waits for them, and re-layouts  5.96 us (4%)
  other arithmetic  3.41 us (2%)
    pallas_call x1, Pallas kernels, body(): pl.pallas_call(functools.partial(kernel, levels, panels, nodes, blocks, w...  139 us
    all_to_all x1, blocking collectives, places(): key = lax.all_to_all(ids, 'panel', split_axis=0, concat_axis=0, tiled=True)  8.98 us
    unnamed x2, local copies, waits for them, and re-layouts  4.62 us

profile of v1, /device:TPU:1, one launch (start us, length us, event | category | flops | bytes accessed | tf_op | source)
XLA Modules:
  0.0 158.4 jit_solution(784232605707170920)
XLA Ops:
  0.6 0.7 subtract_bitcast_fusion
  1.3 0.9 convert_reduce_fusion.1
  2.2 0.7 multiply_add_fusion
  2.9 0.1 select_reduce_fusion.4
  3.0 0.1 sub.26
  3.0 9.0 %all_to_all.6 = s32[8,8,1]{1,2,0:T(1,128)S(1)} all-to-all(s32[8,8,1]{1,2,0:T(1,128)S(1)} %bitcast.6), channel_id=1, replica_groups=mesh['leaf'=4,'panel'=8] {'panel'}, dimensions={0} | all-to-all | bytes 512 | tf_op jit(solution)/shard_map/all_to_all | solution.py:281
  12.0 0.5 broadcast.18
  12.5 0.7 reduce.3
  13.2 0.1 lt.54
  13.3 0.2 select_reduce_fusion.1
  13.5 0.1 select_reduce_fusion.3
  13.6 0.1 select_reduce_fusion
  13.7 0.7 concatenate.3.refs_0_
  14.4 139.4 %shard_map.68 = (f32[1,32,32,256]{3,2,1,0:T(8,128)}, f32[1,32,32,256]{3,2,1,0:T(8,128)}) custom-call(s32[320]{0:T(512)} %concatenate.3.refs_0_, f32[1,32,32,256]{3,2,1,0:T(8,128)} %refs_1_.1, f32[1,32,256,256]{3,2,1,0:T(8,128)} %refs_2_.1, f32[1,32,256,256]{3,2,1,0:T(8,128)} %refs_3_.1), custom_call_target="tpu_custom_call" | custom-call | tf_op jit(solution)/shard_map/pallas_call | solution.py:324
  153.8 2.3 %copy.11 = f32[1,32,32,256]{3,2,1,0:T(8,128)} copy(f32[1,32,32,256]{3,2,1,0:T(8,128)} %get-tuple-element.10) | data formatting | bytes 2097152
  156.1 2.3 %copy.12 = f32[1,32,32,256]{3,2,1,0:T(8,128)} copy(f32[1,32,32,256]{3,2,1,0:T(8,128)} %get-tuple-element.11) | data formatting | bytes 2097152
  (3 shorter events, 0.0 us)

commit v2 on v1

--- a/solution.py
+++ b/solution.py
@@ -10,6 +10,7 @@
 MESH = pl.DeviceIdType.MESH
 ROWS = 8
 WCHUNK = 4
+STAGED = 4
 
 
 def split_rows(x):
@@ -24,18 +25,11 @@
     return out[:ROWS] + out[ROWS:]
 
 
-def times_transposed(x, weights):
-    parts = split_rows(x)
-    out = lax.dot_general(parts, weights, (((1,), (1,)), ((), ())), preferred_element_type=jnp.float32)
-    half = out.shape[1] // 2
-    return (out[:ROWS, :half] + out[ROWS:, :half]) + (out[:ROWS, half:] + out[ROWS:, half:])
-
-
 def kernel(levels, panels, nodes, blocks, width, cap, *refs):
     meta, given, inverse, coupling, fwd_out, bwd_out = refs[:6]
     refs = list(refs[6:])
     take = lambda count: [refs.pop(0) for _ in range(count)]
-    inv32, cpl32, inv, cpl, gbuf, fsol, bsol, upd, prefix, send_up, sums, got_sums, send_down = take(13)
+    inv32, cpl32, inv, cpl, inv_t, cpl_t, gbuf, fsol, bsol, upd, prefix, send_up, sums, got_sums, send_down = take(15)
     got_up, got_down, got_above = take(blocks), take(blocks), take(blocks)
     w_sem, g_sem, o_sem, up_s, up_r, z_s, z_r, dn_s, dn_r, b_s, b_r = take(11)
 
@@ -54,8 +48,9 @@
 
     def weight_copy(which, c):
         source, target = ((inverse, inv32), (coupling, cpl32))[which]
-        span = pl.ds(c * WCHUNK, WCHUNK)
-        return pltpu.make_async_copy(source.at[0, span], target.at[span], w_sem.at[which, c])
+        place = lax.rem(c, STAGED) * WCHUNK
+        return pltpu.make_async_copy(
+            source.at[0, pl.ds(c * WCHUNK, WCHUNK)], target.at[pl.ds(place, WCHUNK)], w_sem.at[which, c])
 
     def out_copy(which, b):
         source, target = ((fsol, fwd_out), (bsol, bwd_out))[which]
@@ -82,7 +77,7 @@
         pltpu.make_async_copy(ref, ref, sem).wait()
 
     given_copy(0).start()
-    for c in range(wchunks):
+    for c in range(min(STAGED, wchunks)):
         weight_copy(0, c).start()
         weight_copy(1, c).start()
     for b in range(1, blocks):
@@ -128,11 +123,16 @@
             for i in range(WCHUNK):
                 n = c * WCHUNK + i
                 for r in range(0, width, 64):
-                    w = source[n, r:r + 64, :]
+                    w = source[lax.rem(c, STAGED) * WCHUNK + i, r:r + 64, :]
                     high = w.astype(jnp.bfloat16)
                     target[n, r:r + 64, :] = high
                     target[n, width + r:width + r + 64, :] = (w - high.astype(jnp.float32)).astype(jnp.bfloat16)
 
+        @pl.when(c + STAGED < wchunks)
+        def _():
+            weight_copy(0, c + STAGED).start()
+            weight_copy(1, c + STAGED).start()
+
         @pl.when(level == 0)
         def _():
             forward_nodes(0, c * WCHUNK, WCHUNK)
@@ -140,6 +140,16 @@
         return carry
 
     lax.fori_loop(0, wchunks, prepare, 0)
+
+    def turn(n, carry):
+        for source, target in ((inv, inv_t), (cpl, cpl_t)):
+            for r in (0, width):
+                target[n, r:r + width, :] = source[n, r:r + width, :].T
+        return carry
+
+    @pl.when(above_bottom)
+    def _():
+        lax.fori_loop(0, nodes, turn, 0)
 
     def forward(b):
         if b > 0:
@@ -196,7 +206,7 @@
                 n = c * chunk + i
                 x = times(gbuf[b, n] - got_sums[b, n], inv[n])
                 fsol[b, n] = x
-                bsol[b, n] = times_transposed(x, inv[n])
+                bsol[b, n] = times(x, inv_t[n])
             down_copy(b, c).start()
             return carry
 
@@ -212,8 +222,8 @@
         def one(c, carry):
             for i in range(chunk):
                 n = c * chunk + i
-                low = times_transposed(got_down[b][meta[m_slot + n]], cpl[n])
-                bsol[b, n] = times_transposed(fsol[b, n] - low, inv[n])
+                low = times(got_down[b][meta[m_slot + n]], cpl_t[n])
+                bsol[b, n] = times(fsol[b, n] - low, inv_t[n])
 
             @pl.when(above_bottom)
             def _():
@@ -238,6 +248,11 @@
                 out_copy(0, b).start()
             if b > 0:
                 add_up(b - 1)
+
+        @pl.when(level == 0)
+        def _():
+            lax.fori_loop(0, nodes, turn, 0)
+
         for b in range(blocks + 1):
             if b < blocks:
                 hand_down(b)
@@ -305,7 +320,8 @@
     dma = pltpu.SemaphoreType.DMA
     chunks = nodes // ROWS
     scratch = [
-        vmem((nodes, width, width), f32), vmem((nodes, width, width), f32),
+        vmem((STAGED * WCHUNK, width, width), f32), vmem((STAGED * WCHUNK, width, width), f32),
+        vmem((nodes, 2 * width, width), bf16), vmem((nodes, 2 * width, width), bf16),
         vmem((nodes, 2 * width, width), bf16), vmem((nodes, 2 * width, width), bf16),
         vmem((blocks, nodes) + tile, f32), vmem((blocks, nodes) + tile, f32), vmem((blocks, nodes) + tile, f32),
         vmem((nodes,) + tile, f32), vmem((slots + 1,) + tile, f32),

time: 159 us -> 147 us (0.925)
  Pallas kernels: 139 us -> 127 us
    pallas_call x1, Pallas kernels: 139 us -> 127 us  [body(): pl.pallas_call(functools.partial(kernel, levels, panels, nodes, blocks, w...]
where the time goes in v2:
time: 147 us; the launch traced here: 146 us
  Pallas kernels  127 us (86%)
  blocking collectives  8.98 us (6%)
  local copies, waits for them, and re-layouts  5.96 us (4%)
  other arithmetic  3.41 us (2%)
    pallas_call x1, Pallas kernels, body(): pl.pallas_call(functools.partial(kernel, levels, panels, nodes, blocks, w...  127 us
    all_to_all x1, blocking collectives, places(): key = lax.all_to_all(ids, 'panel', split_axis=0, concat_axis=0, tiled=True)  8.98 us
    unnamed x2, local copies, waits for them, and re-layouts  4.62 us

profile of v2, /device:TPU:1, one launch (start us, length us, event | category | flops | bytes accessed | tf_op | source)
XLA Modules:
  0.0 146.4 jit_solution(6910868026951373231)
XLA Ops:
  0.6 0.7 subtract_bitcast_fusion
  1.3 0.9 convert_reduce_fusion.1
  2.2 0.7 multiply_add_fusion
  2.9 0.1 select_reduce_fusion.4
  3.0 0.1 sub.26
  3.0 9.0 %all_to_all.6 = s32[8,8,1]{1,2,0:T(1,128)S(1)} all-to-all(s32[8,8,1]{1,2,0:T(1,128)S(1)} %bitcast.6), channel_id=1, replica_groups=mesh['leaf'=4,'panel'=8] {'panel'}, dimensions={0} | all-to-all | bytes 512 | tf_op jit(solution)/shard_map/all_to_all | solution.py:296
  12.0 0.5 broadcast.18
  12.5 0.7 reduce.3
  13.2 0.1 lt.54
  13.3 0.2 select_reduce_fusion.1
  13.5 0.1 select_reduce_fusion.3
  13.6 0.1 select_reduce_fusion
  13.7 0.7 concatenate.3.refs_0_
  14.4 127.4 %shard_map.68 = (f32[1,32,32,256]{3,2,1,0:T(8,128)}, f32[1,32,32,256]{3,2,1,0:T(8,128)}) custom-call(s32[320]{0:T(512)} %concatenate.3.refs_0_, f32[1,32,32,256]{3,2,1,0:T(8,128)} %refs_1_.1, f32[1,32,256,256]{3,2,1,0:T(8,128)} %refs_2_.1, f32[1,32,256,256]{3,2,1,0:T(8,128)} %refs_3_.1), custom_call_target="tpu_custom_call" | custom-call | tf_op jit(solution)/shard_map/pallas_call | solution.py:340
  141.8 2.3 %copy.11 = f32[1,32,32,256]{3,2,1,0:T(8,128)} copy(f32[1,32,32,256]{3,2,1,0:T(8,128)} %get-tuple-element.10) | data formatting | bytes 2097152
  144.1 2.3 %copy.12 = f32[1,32,32,256]{3,2,1,0:T(8,128)} copy(f32[1,32,32,256]{3,2,1,0:T(8,128)} %get-tuple-element.11) | data formatting | bytes 2097152
  (3 shorter events, 0.0 us)
